TPU v7x, 32 devices: a whole 2x2x4 slice. The times are simulated.
32 devices in a mesh: tm: 2 (over x), lat: 8 (over z, y), lon: 2 (over core).
Axes of the slice: x: 2, y: 2, z: 4, core: 2. Of those that a mesh axis runs over, the one named last changes fastest.
Arguments:
- control: bfloat16 [1024, 2, 4, 8, 2048], P('lat', 'tm', None, None, 'lon'), may hold values from -6 to 6
- deviations: float32 [1024, 2, 4, 8, 2048], P('lat', 'tm', None, None, 'lon'), may hold values from 0.3 to 3
- increments: float32 [1024, 2, 4, 8, 2048], P('lat', 'tm', None, None, 'lon'), may hold values from -6 to 6
- lon_corr: bfloat16 [2048, 2048], P('lon'), may hold values from -0.125 to 0.125
- lat_corr: bfloat16 [1024, 1024], P('lat'), may hold values from -0.1875 to 0.1875
- offsets: int32 [2, 8], replicated, may hold values from -2 to 2, as said below
- courant: float32 [4], replicated, may hold values from 0.2 to 0.8
Outputs:
- misfit: float32 [1024, 2, 4, 8, 2048], P('lat', 'tm', None, None, 'lon')
Inputs may be any that keep to these rules, and one draw needn't show every extreme that they name: `offsets`: each of the two rows holds both -2 and 2.
All inputs are finite; a program needn't handle non-finite values.
Results may differ from a plain program's by a relative error of at most 0.0024.
Values may be sent and summed in bfloat16 or wider, within the bound.
A program may use at most 256 MiB of HBM per device.

v0:
```python
import jax
import jax.numpy as jnp
from jax import lax
from jax.sharding import PartitionSpec as P


def with_halo(block, sides, width, periodic):
    for axis, dim in sides:
        count = lax.axis_size(axis)
        forward = [(i, i + 1) for i in range(count - 1)]
        if periodic:
            forward.append((count - 1, 0))
        backward = [(target, source) for source, target in forward]
        low = lax.ppermute(
            lax.slice_in_dim(block, block.shape[dim] - width, None, axis=dim), axis, forward
        )
        high = lax.ppermute(lax.slice_in_dim(block, 0, width, axis=dim), axis, backward)
        block = jnp.concatenate([low, block, high], axis=dim)
    return block


def from_behind(value, axis, steps):
    count = lax.axis_size(axis)
    initial, last = (max(0, -steps), min(count, count - steps))
    return lax.ppermute(value, axis, [(source, source + steps) for source in range(initial, last)])


def advect(field_now, offsets, courant):
    widened = with_halo(field_now.astype(jnp.bfloat16), (("lon", 4),), 2, True).astype(
        field_now.dtype
    )
    padded = with_halo(widened.astype(jnp.bfloat16), (("lat", 0),), 2, False).astype(widened.dtype)
    lat_count = field_now.shape[0]
    lon_count = field_now.shape[4]
    displaced_all = []
    for level_idx in range(field_now.shape[3]):
        one_level = padded[:, :, :, level_idx, :]
        displaced = lax.dynamic_slice_in_dim(one_level, 2 - offsets[0, level_idx], lat_count, 0)
        displaced = lax.dynamic_slice_in_dim(displaced, 2 - offsets[1, level_idx], lon_count, 3)
        displaced_all.append(displaced)
    shifted = jnp.stack(displaced_all, axis=3)
    blending = courant.reshape(1, 1, -1, 1, 1)
    return (1.0 - blending) * field_now + blending * shifted


def body(control, deviations, increments, lon_corr, lat_corr, offsets, courant):
    lat_count = control.shape[0]
    lon_count = control.shape[4]
    flat_rows = control.reshape(-1, lon_count)
    smoothed = lax.dot_general(
        lax.all_gather(flat_rows, "lon", axis=1, tiled=True),
        lon_corr,
        (((1,), (1,)), ((), ())),
        preferred_element_type=jnp.float32,
    )
    halfway = smoothed.astype(jnp.bfloat16).reshape(lat_count, -1)
    full_table = lax.all_gather(lat_corr, "lat", axis=0, tiled=True)
    columns_all = lax.all_to_all(halfway, "lat", split_axis=1, concat_axis=0, tiled=True)
    product = jnp.dot(full_table, columns_all, preferred_element_type=jnp.float32)
    correlated = lax.all_to_all(product, "lat", split_axis=0, concat_axis=1, tiled=True)
    forcing = deviations * correlated.reshape(control.shape)
    evolved = advect(increments, offsets, courant)
    carried = from_behind(evolved, "tm", 1)
    previous = jnp.concatenate([carried, evolved[:, :-1]], axis=1)
    return increments - previous - forcing


def solution(mesh):
    in_specs = (
        P("lat", "tm", None, None, "lon"),
        P("lat", "tm", None, None, "lon"),
        P("lat", "tm", None, None, "lon"),
        P("lon", None),
        P("lat", None),
        P(),
        P(),
    )
    out_specs = P("lat", "tm", None, None, "lon")
    return jax.shard_map(body, mesh=mesh, in_specs=in_specs, out_specs=out_specs, check_vma=False)
```

profile of v0, /device:TPU:18, one launch (start us, length us, event | category | flops | bytes accessed | tf_op | source)
XLA Modules:
  0.0 1222.9 jit_solution(8964060434295330824)
XLA Ops:
  8.1 33.1 %all-gather.3.cloned.1.call-done = bf16[4096,2048]{1,0:T(8,128)(2,1)} async-done(((bf16[4096,1024]{1,0:T(8,128)(2,1)}), bf16[4096,2048]{1,0:T(8,128)(2,1)}) %all-gather.3.cloned.1.call-update) | async-done | bytes 16777232 | tf_op jit(solution)/shard_map/all_gather | solution.py:51
  41.2 23.5 %convolution_convert_fusion = bf16[4096,1024]{1,0:T(8,128)(2,1)} fusion(bf16[4096,2048]{1,0:T(8,128)(2,1)} %all-gather.3.cloned.1.call-done, bf16[1024,2048]{1,0:T(8,128)(2,1)} %param.10), kind=kOutput, calls=%fused_computation.3 | convolution fusion | flops 17184063488 | bytes 29360128 | tf_op jit(solution)/shard_map/dot_general | solution.py:50
  64.7 13.9 %all_to_all.26 = bf16[128,8,4096]{2,1,0:T(8,128)(2,1)} reshape(bf16[4096,1024]{1,0:T(8,128)(2,1)} %convolution_convert_fusion) | data formatting | bytes 16777216 | tf_op jit(solution)/shard_map/all_to_all | solution.py:58
  78.6 11.4 copy.39
  96.6 169.7 %all-gather.5.cloned.1.call-done = bf16[1024,1024]{1,0:T(8,128)(2,1)} async-done(((bf16[128,1024]{1,0:T(8,128)(2,1)}), bf16[1024,1024]{1,0:T(8,128)(2,1)}) %all-gather.5.cloned.1.call-update) | async-done | bytes 2097168 | tf_op jit(solution)/shard_map/all_gather | solution.py:57
  266.2 35.3 %all-to-all-done = bf16[128,8,4096]{2,0,1:T(8,128)(2,1)} async-done(((bf16[128,8,4096]{2,0,1:T(8,128)(2,1)}), bf16[128,8,4096]{2,0,1:T(8,128)(2,1)}, u32[]{:S(2)}, u32[]{:S(2)}) %all-to-all-start) | async-done | bytes 8388640 | tf_op jit(solution)/shard_map/all_to_all | solution.py:58
  301.6 16.1 %fusion.4 = f32[4096,1024]{0,1:T(8,128)} fusion(bf16[1024,1024]{1,0:T(8,128)(2,1)} %all-gather.5.cloned.1.call-done, bf16[1024,4096]{1,0:T(8,128)(2,1)} %bitcast.34), kind=kOutput, calls=%fused_computation.17 | convolution fusion | flops 8589934592 | bytes 27262976 | tf_op jit(solution)/shard_map/dot_general | solution.py:59
  317.7 17.4 %copy.40 = f32[8,128,4096]{1,2,0:T(8,128)} copy(f32[8,128,4096]{2,1,0:T(8,128)} %bitcast.48) | data formatting | bytes 33554432 | tf_op jit(solution)/shard_map/all_to_all | solution.py:60
  335.1 9.0 all-to-all-start.1
  344.1 16.4 %copy.38 = f32[128,1,4,8,1024]{0,4,3,2,1:T(8,128)} copy(f32[128,1,4,8,1024]{4,3,2,1,0:T(8,128)} %param.9) | data formatting | bytes 33554432 | tf_op args[2]
  391.4 54.5 %concatenate.22 = bf16[128,1,4,8,1028]{0,4,3,2,1:T(8,128)(2,1)} concatenate(bf16[128,1,4,8,2]{0,4,3,2,1:T(2,128)(2,1)S(1)} %copy.32, bf16[128,1,4,8,1024]{0,4,3,2,1:T(8,128)(2,1)} %copy-done, bf16[128,1,4,8,2]{0,4,3,2,1:T(2,128)(2,1)S(1)} %copy.33), dimensions={4} | concatenate | bytes 16842752 | tf_op jit(solution)/shard_map/concatenate | solution.py:18
  445.9 13.2 %fusion.1 = (bf16[2,1,4,8,1028]{0,4,3,2,1:T(8,128)(2,1)}, bf16[2,1,4,8,1028]{0,4,3,2,1:T(8,128)(2,1)}) fusion(bf16[128,1,4,8,1028]{0,4,3,2,1:T(8,128)(2,1)} %concatenate.22), kind=kLoop, calls=%fused_computation.14 | loop fusion | bytes 526336 | tf_op jit(solution)/shard_map/slice | solution.py:15
  459.1 7.7 copy.34
  470.1 7.7 copy.35
  481.4 226.9 %collective-permute-done.2 = bf16[2,1,4,8,1028]{4,3,2,1,0:T(8,128)(2,1)S(1)} collective-permute-done((bf16[2,1,4,8,1028]{4,3,2,1,0:T(8,128)(2,1)S(1)}, bf16[2,1,4,8,1028]{4,3,2,1,0:T(8,128)(2,1)S(1)}, u32[]{:S(2)}, u32[]{:S(2)}) %collective-permute-start.2) | collective-permute-done | bytes 131616 | tf_op jit(solution)/shard_map/ppermute | solution.py:14
  708.2 6.7 copy.36
  715.0 6.7 copy.37
  721.7 23.4 %maximum_convert_fusion = f32[132,1,4,8,1028]{0,4,3,2,1:T(8,128)} fusion(bf16[2,1,4,8,1028]{0,4,3,2,1:T(8,128)(2,1)} %copy.37, bf16[128,1,4,8,1028]{0,4,3,2,1:T(8,128)(2,1)} %concatenate.22, bf16[2,1,4,8,1028]{0,4,3,2,1:T(8,128)(2,1)} %copy.36), kind=kLoop, calls=%fused_computation | loop fusion | flops 26053632 | bytes 26053632 | tf_op jit(solution)/shard_map/convert_element_type | solution.py:32
  745.1 20.9 %fusion = (f32[132,1,4,1,1028]{0,4,3,2,1:T(8,128)S(1)}, f32[132,1,4,1,1028]{0,4,3,2,1:T(8,128)S(1)}, f32[132,1,4,1,1028]{0,4,3,2,1:T(8,128)}, f32[132,1,4,1,1028...) fusion(f32[132,1,4,8,1028]{0,4,3,2,1:T(8,128)} %maximum_convert, ...), kind=kLoop, calls=%fused_computation.13 | loop fusion | bytes 34738176 | tf_op jit(solution)/shard_map/slice | solution.py:37
  795.1 11.9 multiply_add_fusion
  808.4 16.4 %copy.41 = f32[128,1,4,8,1024]{0,4,3,2,1:T(8,128)} copy(f32[128,1,4,8,1024]{4,3,2,1,0:T(8,128)} %param.8) | data formatting | bytes 33554432 | tf_op args[1]
  824.8 346.6 %collective-permute-done.4 = f32[128,1,4,8,1024]{0,4,3,2,1:T(8,128)} collective-permute-done((f32[128,1,4,8,1024]{0,4,3,2,1:T(8,128)}, f32[128,1,4,8,1024]{0,4,3,2,1:T(8,128)}, u32[]{:S(2)}, u32[]{:S(2)}) %collective-permute-start.4) | collective-permute-done | bytes 16777248 | tf_op jit(solution)/shard_map/ppermute | solution.py:25
  1171.4 27.5 %multiply_subtract_fusion = f32[128,1,4,8,1024]{0,4,3,2,1:T(8,128)} fusion(f32[128,1,4,8,1024]{0,4,3,2,1:T(8,128)} %copy.41, f32[128,1,4,8,1024]{0,4,3,2,1:T(8,128)} %bitcast.38, f32[128,1,4,8,1024]{0,4,3,2,1:T(8,128)} %copy.38, f32[128,1,4,8,1024]{0,4,3,2,1:T(8,128)} %collective-permute-done.4), kind=kLoop, calls=%fused_computation.1 | loop fusion | flops 12582912 | bytes 83886080 | tf_op jit(solution)/shard_map/sub | solution.py:65
  1199.0 16.5 %copy.42 = f32[128,1,4,8,1024]{4,3,2,1,0:T(8,128)} copy(f32[128,1,4,8,1024]{0,4,3,2,1:T(8,128)} %multiply_subtract_fusion) | data formatting | bytes 33554432 | tf_op jit(solution)/shard_map/sub | solution.py:65
  (45 shorter events, 55.7 us)
Async XLA Ops:
  7.4 33.8 %all-gather.3.cloned.1.call-start = ((), (), s32[]{:S(2)}) async-start(), calls=%async_computation.2 | async-start | bytes 25165824 | tf_op jit(solution)/shard_map/all_gather | solution.py:51
  90.0 211.6 %all-to-all-start = ((bf16[128,8,4096]{2,0,1:T(8,128)(2,1)}), bf16[128,8,4096]{2,0,1:T(8,128)(2,1)}, u32[]{:S(2)}, u32[]{:S(2)}) async-start(bf16[128,8,4096]{2,0,1:T(8,128)(2,1)} %copy.39), calls=%async_computation | async-start | bytes 16777216 | tf_op jit(solution)/shard_map/all_to_all | solution.py:58
  96.0 170.2 %all-gather.5.cloned.1.call-start = ((), (), s32[]{:S(2)}) async-start(), calls=%async_computation.3 | async-start | bytes 2359296 | tf_op jit(solution)/shard_map/all_gather | solution.py:57
  335.1 836.3 %all-to-all-start.1 = ((f32[8,128,4096]{1,2,0:T(8,128)}), f32[8,128,4096]{1,2,0:T(8,128)}, u32[]{:S(2)}, u32[]{:S(2)}) async-start(f32[8,128,4096]{1,2,0:T(8,128)} %copy.40), calls=%async_computation.1 | async-start | bytes 33554432 | tf_op jit(solution)/shard_map/all_to_all | solution.py:60
  360.6 10.4 copy-start.1
  367.1 3.3 copy-start
  370.4 21.0 %collective-permute-start = (bf16[128,1,4,8,2]{0,3,4,2,1:T(8,128)(2,1)S(1)}, bf16[128,1,4,8,2]{0,3,4,2,1:T(8,128)(2,1)S(1)}, u32[]{:S(2)}, u32[]{:S(2)}) collective-permute-start(bf16[128,1,4,8,2]{0,3,4,2,1:T(8,128)(2,1)S(1)} %copy.30), channel_id=1, source_target_pairs={{0,1},{1,0},{2,3},{3,2},{4,5},{5,4},{6,7},{7,6},{8,9},{9,8},{10,11... | collective-permute-start | bytes 49160 | tf_op jit(solution)/shard_map/ppermute | solution.py:14
  370.5 20.9 %collective-permute-start.1 = (bf16[128,1,4,8,2]{0,3,4,2,1:T(8,128)(2,1)S(1)}, bf16[128,1,4,8,2]{0,3,4,2,1:T(8,128)(2,1)S(1)}, u32[]{:S(2)}, u32[]{:S(2)}) collective-permute-start(bf16[128,1,4,8,2]{0,3,4,2,1:T(8,128)(2,1)S(1)} %copy.31), channel_id=1, source_target_pairs={{1,0},{0,1},{3,2},{2,3},{5,4},{4,5},{7,6},{6,7},{9,8},{8,9},{11,10... | collective-permute-start | bytes 49160 | tf_op jit(solution)/shard_map/ppermute | solution.py:17
  459.0 22.3 %copy-start.2 = (f32[4]{0:T(128)S(1)}, f32[4]{0:T(128)}, u32[]{:S(2)}) copy-start(f32[4]{0:T(128)} %param.13) | copy-start | bytes 52
  466.7 241.5 %collective-permute-start.2 = (bf16[2,1,4,8,1028]{4,3,2,1,0:T(8,128)(2,1)S(1)}, bf16[2,1,4,8,1028]{4,3,2,1,0:T(8,128)(2,1)S(1)}, u32[]{:S(2)}, u32[]{:S(2)}) collective-permute-start(bf16[2,1,4,8,1028]{4,3,2,1,0:T(8,128)(2,1)S(1)} %copy.34), channel_id=1, source_target_pairs={{0,2},{2,4},{4,6},{6,8},{8,10},{10,12},{12,14},{1,3},{3,5},{5,7},{... | collective-permute-start | bytes 394760 | tf_op jit(solution)/shard_map/ppermute | solution.py:14
  477.8 237.2 %collective-permute-start.3 = (bf16[2,1,4,8,1028]{4,3,2,1,0:T(8,128)(2,1)S(1)}, bf16[2,1,4,8,1028]{4,3,2,1,0:T(8,128)(2,1)S(1)}, u32[]{:S(2)}, u32[]{:S(2)}) collective-permute-start(bf16[2,1,4,8,1028]{4,3,2,1,0:T(8,128)(2,1)S(1)} %copy.35), channel_id=1, source_target_pairs={{2,0},{4,2},{6,4},{8,6},{10,8},{12,10},{14,12},{3,1},{5,3},{7,5},{... | collective-permute-start | bytes 394760 | tf_op jit(solution)/shard_map/ppermute | solution.py:17
  766.0 29.1 %slice-start = ((s8[16777216]{0:T(1024)(128)(4,1)}), s8[4194304]{0:T(1024)(128)(4,1)S(1)}, s32[]{:S(2)}) async-start(s8[16777216]{0:T(1024)(128)(4,1)} %bitcast.46), calls=%async_computation.4 | async-start | bytes 8388608
  774.5 20.7 %slice-start.1 = ((s8[16777216]{0:T(1024)(128)(4,1)}), s8[4194304]{0:T(1024)(128)(4,1)S(1)}, s32[]{:S(2)}) async-start(s8[16777216]{0:T(1024)(128)(4,1)} %bitcast.46), calls=%async_computation.5 | async-start | bytes 8388608
  782.9 12.3 %slice-start.2 = ((s8[16777216]{0:T(1024)(128)(4,1)}), s8[4194304]{0:T(1024)(128)(4,1)S(1)}, s32[]{:S(2)}) async-start(s8[16777216]{0:T(1024)(128)(4,1)} %bitcast.46), calls=%async_computation.6 | async-start | bytes 8388608
  791.3 3.9 slice-start.3
  807.1 364.3 %collective-permute-start.4 = (f32[128,1,4,8,1024]{0,4,3,2,1:T(8,128)}, f32[128,1,4,8,1024]{0,4,3,2,1:T(8,128)}, u32[]{:S(2)}, u32[]{:S(2)}) collective-permute-start(f32[128,1,4,8,1024]{0,4,3,2,1:T(8,128)} %multiply_add_fusion), channel_id=1, source_target_pairs={{0,16},{1,17},{2,18},{3,19},{4,20},{5,21},{6,22},{7,23},{8,24},{9,... | collective-permute-start | bytes 50331656 | tf_op jit(solution)/shard_map/ppermute | solution.py:25
Sparse Core Ops, SparseCore 0:
  9.7 31.3 all-gather.2
Sparse Core Ops, SparseCore 1:
  98.6 167.6 all-gather.4
where the time goes:
time: 1230 us; the launch traced here: 1220 us
  waiting for transfers between devices  813 us (66%)
  local copies, waits for them, and re-layouts  243 us (20%)
  other arithmetic  69.4 us (6%)
  matrix products  39.6 us (3%)
  between operations  34.7 us (3%)
  starting transfers between devices  23.9 us (2%)
    ppermute x1, waiting for transfers between devices, from_behind(): lax.ppermute(value, axis, [(source, source + steps) for source in range(i...  347 us
    ppermute x2, waiting for transfers between devices, with_halo(): lax.ppermute(lax.slice_in_dim(block, block.shape[dim] - width, None, axis...  227 us
    all_gather x1, waiting for transfers between devices, body(): full_table = lax.all_gather(lat_corr, 'lat', axis=0, tiled=True)  170 us
    unnamed x23, local copies, waits for them, and re-layouts  63.3 us
    concatenate x1, local copies, waits for them, and re-layouts, with_halo(): block = jnp.concatenate([low, block, high], axis=dim)  54.5 us
    all_to_all x1, waiting for transfers between devices, body(): lax.all_to_all(halfway, 'lat', split_axis=1, concat_axis=0, tiled=True)  35.3 us
    all_gather x1, waiting for transfers between devices, body(): lax.all_gather(flat_rows, 'lon', axis=1, tiled=True)  33.1 us
    sub x1, other arithmetic, body(): return increments - previous - forcing  27.5 us
  transfers between devices with their start and end apart: 9, of which 5 were waited for; matrix products, arithmetic and copies ran while one was open for 18% of the time, Pallas kernels for 0%

commit v1 on v0

--- a/solution.py
+++ b/solution.py
@@ -1,6 +1,8 @@
 import jax
 import jax.numpy as jnp
 from jax import lax
+from jax.experimental import pallas as pl
+from jax.experimental.pallas import tpu as pltpu
 from jax.sharding import PartitionSpec as P
 
 
@@ -43,7 +45,7 @@
     return (1.0 - blending) * field_now + blending * shifted
 
 
-def body(control, deviations, increments, lon_corr, lat_corr, offsets, courant):
+def lat_columns(control, deviations, increments, lon_corr, lat_corr, offsets, courant):
     lat_count = control.shape[0]
     lon_count = control.shape[4]
     flat_rows = control.reshape(-1, lon_count)
@@ -65,6 +67,202 @@
     return increments - previous - forcing
 
 
+LIMIT = 48 * 1024 * 1024
+
+
+def cost(flops, nbytes):
+    return pl.CostEstimate(flops=flops, bytes_accessed=nbytes, transcendentals=0)
+
+
+def row_block(rows, largest):
+    block = min(rows, largest)
+    while rows % block:
+        block -= 16
+    return block
+
+
+def fields_first(control, first, count):
+    rows, nvar, levels, lons = control.shape
+    block = row_block(rows, 64)
+
+    def kernel(x_ref, y_ref):
+        y_ref[0] = jnp.swapaxes(x_ref[:, 0].astype(jnp.float32), 0, 1).astype(jnp.bfloat16)
+
+    return pl.pallas_call(
+        kernel,
+        grid=(count, rows // block),
+        in_specs=[pl.BlockSpec((block, 1, levels, lons), lambda v, r: (r, first + v, 0, 0))],
+        out_specs=pl.BlockSpec((1, levels, block, lons), lambda v, r: (v, 0, r, 0)),
+        out_shape=jax.ShapeDtypeStruct((count, levels, rows, lons), jnp.bfloat16),
+        compiler_params=pltpu.CompilerParams(vmem_limit_bytes=LIMIT),
+        cost_estimate=cost(0, 4 * count * levels * rows * lons),
+        name="fields_first",
+    )(control)
+
+
+def evolve(increments, padded, offsets, courant):
+    rows, nvar, levels, lons = increments.shape
+    wide = padded.shape[-1]
+    rim = (wide - lons) // 2
+    block = row_block(rows, 32)
+
+    def kernel(off_ref, cour_ref, inc_ref, pad_ref, out_ref):
+        weight = cour_ref[pl.program_id(0)]
+        start = pl.program_id(1) * block
+        lat_off, lon_off = off_ref[:, 0:1], off_ref[:, 1:2]
+
+        def one(i, carry):
+            row = jnp.zeros((levels, wide), jnp.float32)
+            for step in range(-2, 3):
+                source = pad_ref[start + i + 2 - step, 0].astype(jnp.float32)
+                row = jnp.where(lat_off == step, source, row)
+            moved = jnp.zeros((levels, lons), jnp.float32)
+            for step in range(-2, 3):
+                rolled = pltpu.roll(row, step % wide, 1) if step else row
+                moved = jnp.where(lon_off == step, rolled[:, rim : rim + lons], moved)
+            mixed = (1.0 - weight) * inc_ref[i, 0] + weight * moved
+            out_ref[i, 0] = mixed.astype(jnp.bfloat16)
+            return carry
+
+        lax.fori_loop(0, block, one, 0)
+
+    return pl.pallas_call(
+        kernel,
+        grid=(nvar, rows // block),
+        in_specs=[
+            pl.BlockSpec((levels, 2), lambda v, r: (0, 0)),
+            pl.BlockSpec(memory_space=pltpu.SMEM),
+            pl.BlockSpec((block, 1, levels, lons), lambda v, r: (r, v, 0, 0)),
+            pl.BlockSpec((rows + 4, 1, levels, wide), lambda v, r: (0, v, 0, 0)),
+        ],
+        out_specs=pl.BlockSpec((block, 1, levels, lons), lambda v, r: (r, v, 0, 0)),
+        out_shape=jax.ShapeDtypeStruct(increments.shape, jnp.bfloat16),
+        compiler_params=pltpu.CompilerParams(vmem_limit_bytes=LIMIT),
+        cost_estimate=cost(30 * increments.size, 8 * increments.size),
+        name="evolve",
+    )(offsets.T, courant, increments, padded)
+
+
+def residual(increments, deviations, previous, correlated, first, count, filled):
+    rows, nvar, levels, lons = increments.shape
+    block = row_block(rows, 32)
+
+    def kernel(inc_ref, dev_ref, prev_ref, corr_ref, *others):
+        out_ref = others[-1]
+        corr = jnp.swapaxes(corr_ref[0].astype(jnp.float32), 0, 1)
+        out_ref[:, 0] = (
+            inc_ref[:, 0] - prev_ref[:, 0].astype(jnp.float32) - dev_ref[:, 0] * corr
+        )
+
+    spec = pl.BlockSpec((block, 1, levels, lons), lambda v, r: (r, first + v, 0, 0))
+    in_specs = [spec] * 3 + [
+        pl.BlockSpec((1, levels, block, lons), lambda v, r: (v, 0, r, 0))
+    ]
+    operands = [increments, deviations, previous, correlated]
+    aliases = {}
+    if filled is not None:
+        in_specs.append(pl.BlockSpec(memory_space=pl.ANY))
+        operands.append(filled)
+        aliases = {4: 0}
+    return pl.pallas_call(
+        kernel,
+        grid=(count, rows // block),
+        in_specs=in_specs,
+        out_specs=spec,
+        out_shape=jax.ShapeDtypeStruct(increments.shape, jnp.float32),
+        input_output_aliases=aliases,
+        compiler_params=pltpu.CompilerParams(vmem_limit_bytes=LIMIT),
+        cost_estimate=cost(6 * count * levels * rows * lons, 16 * count * levels * rows * lons),
+        name="residual",
+    )(*operands)
+
+
+def swap(value, axis, steps, periodic):
+    count = lax.axis_size(axis)
+    pairs = [(i, i + steps) for i in range(count) if 0 <= i + steps < count]
+    if periodic:
+        pairs = [(i, (i + steps) % count) for i in range(count)]
+    return lax.ppermute(value, axis, pairs)
+
+
+def widen(field, rim):
+    lons = field.shape[-1]
+    low = swap(field[..., lons - rim :], "lon", 1, True)
+    high = swap(field[..., :rim], "lon", -1, True)
+    wide = jnp.concatenate([low, field, high], axis=-1)
+    below = swap(wide[-2:], "lat", 1, False)
+    above = swap(wide[:2], "lat", -1, False)
+    return jnp.concatenate([below, wide, above], axis=0)
+
+
+def gathered_table(lat_corr):
+    sharers = lax.axis_size("tm") * lax.axis_size("lon")
+    width = lat_corr.shape[1] // sharers
+    mine = lax.axis_index("tm") * lax.axis_size("lon") + lax.axis_index("lon")
+    piece = lax.dynamic_slice_in_dim(lat_corr, mine * width, width, 1)
+    piece = lax.all_gather(piece, "lat", axis=0, tiled=True)
+    return lax.all_gather(piece, ("tm", "lon"), axis=1, tiled=True)
+
+
+def whole_fields(control, deviations, increments, lon_corr, lat_corr, offsets, courant):
+    rows, _, nvar, levels, lons = control.shape
+    n_lat, n_lon = lax.axis_size("lat"), lax.axis_size("lon")
+    group = n_lat * n_lon
+    rounds = nvar * levels // group
+    vars_each = nvar // rounds
+    flat = (rows, nvar, levels, lons)
+    control, deviations, increments = (
+        x.reshape(flat) for x in (control, deviations, increments)
+    )
+    sent = []
+    for k in range(rounds):
+        block = fields_first(control, k * vars_each, vars_each).reshape(group, rows, lons)
+        sent.append(
+            lax.all_to_all(block, ("lat", "lon"), split_axis=0, concat_axis=0, tiled=True)
+        )
+    full_lon = lax.all_gather(lon_corr, "lon", axis=0, tiled=True)
+    full_lat = gathered_table(lat_corr)
+    padded = widen(increments.astype(jnp.bfloat16), 128)
+    evolved = evolve(increments, padded, offsets, courant)
+    previous = lax.ppermute(evolved, "tm", [(i, i + 1) for i in range(lax.axis_size("tm") - 1)])
+    back = []
+    for k in range(rounds):
+        field = sent[k].reshape(n_lat, n_lon, rows, lons).transpose(0, 2, 1, 3)
+        field = field.reshape(n_lat * rows, n_lon * lons)
+        smoothed = lax.dot_general(
+            field, full_lon, (((1,), (1,)), ((), ())), preferred_element_type=jnp.float32
+        ).astype(jnp.bfloat16)
+        product = jnp.dot(full_lat, smoothed, preferred_element_type=jnp.float32)
+        product = product.astype(jnp.bfloat16).reshape(n_lat, rows, n_lon, lons)
+        product = product.transpose(0, 2, 1, 3).reshape(group, rows, lons)
+        back.append(
+            lax.all_to_all(product, ("lat", "lon"), split_axis=0, concat_axis=0, tiled=True)
+        )
+    out = None
+    for k in range(rounds):
+        correlated = back[k].reshape(vars_each, levels, rows, lons)
+        out = residual(
+            increments, deviations, previous, correlated, k * vars_each, vars_each, out
+        )
+    return out.reshape(rows, 1, nvar, levels, lons)
+
+
+def body(control, deviations, increments, lon_corr, lat_corr, offsets, courant):
+    rows, slots, nvar, levels, lons = control.shape
+    group = lax.axis_size("lat") * lax.axis_size("lon")
+    sharers = lax.axis_size("tm") * lax.axis_size("lon")
+    arrays = (control, deviations, increments, lon_corr, lat_corr, offsets, courant)
+    fits = (
+        slots == 1
+        and (nvar * levels) % group == 0
+        and group % levels == 0
+        and rows % 16 == 0
+        and lons % 128 == 0
+        and lat_corr.shape[1] % (128 * sharers) == 0
+    )
+    return whole_fields(*arrays) if fits else lat_columns(*arrays)
+
+
 def solution(mesh):
     in_specs = (
         P("lat", "tm", None, None, "lon"),

time: 1230 us -> 664 us (0.54)
  waiting for transfers between devices: 813 us -> 271 us
  local copies, waits for them, and re-layouts: 243 us -> 49.1 us
  Pallas kernels: 0 us -> 128 us
  blocking collectives: 0 us -> 114 us
  other arithmetic: 69.4 us -> 18.5 us
  between operations: 34.7 us -> 13.6 us
    ppermute x5, waiting for transfers between devices: 573 us -> 228 us  [the longest x1 140 us: whole_fields(): lax.ppermute(evolved, 'tm', [(i, i + 1) for i in range(lax.axis_size('tm'...]
    all_gather x2, waiting for transfers between devices: 203 us -> 13.5 us  [the longest x1 13.5 us: whole_fields(): full_lon = lax.all_gather(lon_corr, 'lon', axis=0, tiled=True)]
    pallas_call x0 -> x5, Pallas kernels: none -> 128 us  [the longest x1 91.8 us: evolve(): pl.pallas_call(kernel, grid=(nvar, rows // block), in_specs=[pl.BlockSpec...]
    all_gather x0 -> x1, blocking collectives: none -> 114 us  [gathered_table(): piece = lax.all_gather(piece, 'lat', axis=0, tiled=True)]
    unnamed x23 -> x17, local copies, waits for them, and re-layouts: 63.3 us -> 7.53 us
    concatenate x1 -> x0, local copies, waits for them, and re-layouts: 54.5 us -> none  [with_halo(): block = jnp.concatenate([low, block, high], axis=dim)]
    slice x8 -> x1, local copies, waits for them, and re-layouts: 50.2 us -> 1.39 us  [widen(): low = swap(field[..., lons - rim:], 'lon', 1, True)]
    all_to_all x3 -> x0, local copies, waits for them, and re-layouts: 42.7 us -> none  [the longest x2 25.3 us: body(): lax.all_to_all(halfway, 'lat', split_axis=1, concat_axis=0, tiled=True)]
  transfers between devices with their start and end apart: 9 -> 11, of which waited for: 5 -> 4; matrix products, arithmetic and copies ran while one was open for 18% -> 15% of each run, Pallas kernels for 0% -> 17%
where the time goes in v1:
time: 664 us; the launch traced here: 663 us
  waiting for transfers between devices  271 us (41%)
  Pallas kernels  128 us (19%)
  blocking collectives  114 us (17%)
  local copies, waits for them, and re-layouts  49.1 us (7%)
  matrix products  37.2 us (6%)
  starting transfers between devices  31.8 us (5%)
  other arithmetic  18.5 us (3%)
  between operations  13.6 us (2%)
    ppermute x1, waiting for transfers between devices, whole_fields(): lax.ppermute(evolved, 'tm', [(i, i + 1) for i in range(lax.axis_size('tm'...  140 us
    all_gather x1, blocking collectives, gathered_table(): piece = lax.all_gather(piece, 'lat', axis=0, tiled=True)  114 us
    pallas_call x1, Pallas kernels, evolve(): pl.pallas_call(kernel, grid=(nvar, rows // block), in_specs=[pl.BlockSpec...  91.8 us
    ppermute x4, waiting for transfers between devices, swap(): return lax.ppermute(value, axis, pairs)  88.1 us
    dot_general x2, matrix products, whole_fields(): product = jnp.dot(full_lat, smoothed, preferred_element_type=jnp.float32)  37.2 us
    all_to_all x2, waiting for transfers between devices, whole_fields(): lax.all_to_all(block, ('lat', 'lon'), split_axis=0, concat_axis=0, tiled=...  28.3 us
    pallas_call x2, Pallas kernels, residual(): pl.pallas_call(kernel, grid=(count, rows // block), in_specs=in_specs, ou...  27 us
    reshape x2, local copies, waits for them, and re-layouts, whole_fields(): product = product.astype(jnp.bfloat16).reshape(n_lat, rows, n_lon, lons)  15.6 us
  transfers between devices with their start and end apart: 11, of which 4 were waited for; matrix products, arithmetic and copies ran while one was open for 15% of the time, Pallas kernels for 17%

profile of v1, /device:TPU:18, one launch (start us, length us, event | category | flops | bytes accessed | tf_op | source)
XLA Modules:
  0.0 662.6 jit_solution(7235773743322778954)
XLA Ops:
  6.5 4.5 fields_first.3
  13.1 6.2 all-to-all-start.2
  19.4 113.9 %all_gather.9 = bf16[1024,256]{1,0:T(8,128)(2,1)} all-gather(bf16[128,256]{1,0:T(8,128)(2,1)S(1)} %constant_dynamic-slice_fusion), channel_id=1, replica_groups=mesh['tm'=2,'lat'=8,'lon'=2] {'lat'}, dimensions={0}, use_global_device_ids=true | all-gather | bytes 589824 | tf_op jit(solution)/shard_map/all_gather | solution.py:203
  134.1 4.5 fields_first.2
  140.7 7.4 %all-to-all-start = ((bf16[16,128,1024]{2,1,0:T(8,128)(2,1)}), bf16[16,128,1024]{2,1,0:T(8,128)(2,1)}, u32[]{:S(2)}, u32[]{:S(2)}) async-start(bf16[16,128,1024]{2,1,0:T(8,128)(2,1)} %bitcast.53), calls=%async_computation | async-start | bytes 8388608 | tf_op jit(solution)/shard_map/all_to_all | solution.py:221
  148.1 6.6 bitcast_convert_fusion
  160.0 6.8 %copy.20 = bf16[8,128,2,1024]{1,0,3,2:T(8,128)(2,1)} copy(bf16[8,128,2,1024]{3,1,2,0:T(8,128)(2,1)} %bitcast.12) | data formatting | bytes 8388608 | tf_op jit(solution)/shard_map/transpose | solution.py:230
  166.7 13.5 %all-gather.5.cloned.1.call-done = bf16[2048,2048]{1,0:T(8,128)(2,1)} async-done(((bf16[1024,2048]{1,0:T(8,128)(2,1)}), bf16[2048,2048]{1,0:T(8,128)(2,1)}) %all-gather.5.cloned.1.call-update) | async-done | bytes 8388624 | tf_op jit(solution)/shard_map/all_gather | solution.py:223
  180.3 18.9 %fusion.23 = bf16[1024,2048]{1,0:T(8,128)(2,1)} fusion(bf16[1024,1024]{1,0:T(8,128)(2,1)} %all-gather.3.cloned.1.call-done, bf16[2048,2048]{1,0:T(8,128)(2,1)} %all-gather.5.cloned.1.call-done, bf16[256,8,8,128]{3,2,1,0:T(8,128)(2,1)} %bitcast.66), kind=kOutput, calls=%fused_computation.12 | convolution fusion | flops 12889096192 | bytes 18874368 | tf_op jit(solution)/shard_map/dot_general | solution.py:235
  199.1 7.8 %reshape.60 = bf16[8,128,2,1024]{3,2,1,0:T(2,128)(2,1)} reshape(bf16[1024,2048]{1,0:T(8,128)(2,1)} %fusion.23) | data formatting | bytes 8388608 | tf_op jit(solution)/shard_map/reshape | solution.py:236
  206.9 5.6 copy.21
  212.5 28.3 %all-to-all-done = bf16[16,128,1024]{2,1,0:T(8,128)(2,1)} async-done(((bf16[16,128,1024]{2,1,0:T(8,128)(2,1)}), bf16[16,128,1024]{2,1,0:T(8,128)(2,1)}, u32[]{:S(2)}, u32[]{:S(2)}) %all-to-all-start) | async-done | bytes 4194336 | tf_op jit(solution)/shard_map/all_to_all | solution.py:221
  240.8 4.8 all-to-all-start.3
  253.7 88.0 %collective-permute-done.2 = bf16[2,4,8,1280]{3,2,1,0:T(8,128)(2,1)S(1)} collective-permute-done((bf16[2,4,8,1280]{3,2,1,0:T(8,128)(2,1)S(1)}, bf16[2,4,8,1280]{3,2,1,0:T(8,128)(2,1)S(1)}, u32[]{:S(2)}, u32[]{:S(2)}) %collective-permute-start.2) | collective-permute-done | bytes 163872 | tf_op jit(solution)/shard_map/ppermute | solution.py:185
  341.7 10.9 %pad_maximum_fusion.pad_ref = bf16[132,4,8,1280]{3,2,1,0:T(8,128)(2,1)} fusion(bf16[2,4,8,1280]{3,2,1,0:T(8,128)(2,1)S(1)} %collective-permute-done.3, bf16[128,4,8,128]{3,2,1,0:T(8,128)(2,1)S(1)} %collective-permute-done.1, bf16[128,4,8,1024]{3,2,1,0:T(8,128)(2,1)} %copy-done.5, bf16[128,4,8,128]{3,2,1,0:T(8,128)(2,1)S(1)} %collective-permute-done, ...), kind=kLoop, calls=%fused_computation | loop fusion | flops 54067200 | bytes 21626880 | tf_op jit(solution)/shard_map/concatenate | solution.py:195
  352.6 91.8 %evolve.1 = bf16[128,4,8,1024]{3,2,1,0:T(8,128)(2,1)} custom-call(s32[8,2]{1,0:T(8,128)S(1)} %bitcast.54, f32[4]{0:T(128)S(1)} %copy-done.4, f32[128,4,8,1024]{3,2,1,0:T(8,128)} %bitcast.55, bf16[132,4,8,1280]{3,2,1,0:T(8,128)(2,1)} %pad_maximum_fusion.pad_ref), custom_call_target="tpu_custom_call" | custom-call | flops 125829120 | bytes 33554432 | tf_op jit(solution)/shard_map/evolve/pallas_call | solution.py:129
  445.9 6.8 %copy.18 = bf16[8,128,2,1024]{1,0,3,2:T(8,128)(2,1)} copy(bf16[8,128,2,1024]{3,1,2,0:T(8,128)(2,1)} %bitcast.6) | data formatting | bytes 8388608 | tf_op jit(solution)/shard_map/transpose | solution.py:230
  452.6 18.3 %fusion.18 = bf16[1024,2048]{1,0:T(8,128)(2,1)} fusion(bf16[1024,1024]{1,0:T(8,128)(2,1)S(1)} %copy-done.7, bf16[2048,2048]{1,0:T(8,128)(2,1)} %all-gather.5.cloned.1.call-done, bf16[256,8,8,128]{3,2,1,0:T(8,128)(2,1)} %bitcast.67), kind=kOutput, calls=%fused_computation.11 | convolution fusion | flops 12889096192 | bytes 18874368 | tf_op jit(solution)/shard_map/dot_general | solution.py:235
  470.9 7.8 %reshape.54 = bf16[8,128,2,1024]{3,2,1,0:T(2,128)(2,1)} reshape(bf16[1024,2048]{1,0:T(8,128)(2,1)} %fusion.18) | data formatting | bytes 8388608 | tf_op jit(solution)/shard_map/reshape | solution.py:236
  478.7 5.5 copy.19
  484.2 4.5 all-to-all-start.1
  488.6 140.1 %collective-permute-done.4.prev_ref = bf16[128,4,8,1024]{3,2,1,0:T(8,128)(2,1)} collective-permute-done((bf16[128,4,8,1024]{3,2,1,0:T(8,128)(2,1)}, bf16[128,4,8,1024]{3,2,1,0:T(8,128)(2,1)}, u32[]{:S(2)}, u32[]{:S(2)}) %collective-permute-start.4) | collective-permute-done | bytes 8388640 | tf_op jit(solution)/shard_map/ppermute | solution.py:227
  628.8 13.4 %residual.2.others_0_ = f32[128,4,8,1024]{3,2,1,0:T(8,128)} custom-call(f32[128,4,8,1024]{3,2,1,0:T(8,128)} %bitcast.56, f32[128,4,8,1024]{3,2,1,0:T(8,128)} %bitcast.58, bf16[128,4,8,1024]{3,2,1,0:T(8,128)(2,1)} %collective-permute-done.4.prev_ref, bf16[2,8,128,1024]{3,2,1,0:T(8,128)(2,1)} %bitcast.15.corr_ref), custom_call_target="tpu_custom_call" | custom-call | flops 12582912 | bytes 33554432 | tf_op jit(solution)/shard_map/residual/pallas_call | solution.py:167
  642.2 13.5 %residual.3 = f32[128,4,8,1024]{3,2,1,0:T(8,128)} custom-call(f32[128,4,8,1024]{3,2,1,0:T(8,128)} %bitcast.57, f32[128,4,8,1024]{3,2,1,0:T(8,128)} %bitcast.59, bf16[128,4,8,1024]{3,2,1,0:T(8,128)(2,1)} %collective-permute-done.4.prev_ref, bf16[2,8,128,1024]{3,2,1,0:T(8,128)(2,1)} %bitcast.9.corr_ref, ...), custom_call_target="tpu_custom_call", output_to_operand_aliasing={{}: (4, {})} | custom-call | flops 12582912 | bytes 33554432 | tf_op jit(solution)/shard_map/residual/pallas_call | solution.py:167
  (36 shorter events, 19.6 us)
Async XLA Ops:
  6.5 12.8 %copy-start = (bf16[128,1024]{1,0:T(8,128)(2,1)S(1)}, bf16[128,1024]{1,0:T(8,128)(2,1)}, u32[]{:S(2)}) copy-start(bf16[128,1024]{1,0:T(8,128)(2,1)} %param.11) | copy-start | bytes 786436
  11.1 2.1 copy-start.2
  13.1 127.5 %all-to-all-start.2 = ((bf16[16,128,1024]{2,1,0:T(8,128)(2,1)}), bf16[16,128,1024]{2,1,0:T(8,128)(2,1)}, u32[]{:S(2)}, u32[]{:S(2)}) async-start(bf16[16,128,1024]{2,1,0:T(8,128)(2,1)} %bitcast.52), calls=%async_computation.2 | async-start | bytes 8388608 | tf_op jit(solution)/shard_map/all_to_all | solution.py:221
  19.3 147.4 %all-gather.3.cloned.1.call-start = ((), (), s32[]{:S(2)}) async-start(), calls=%async_computation.4 | async-start | bytes 2621440 | tf_op jit(solution)/shard_map/all_gather | solution.py:204
  133.4 46.9 %all-gather.5.cloned.1.call-start = ((), (), s32[]{:S(2)}) async-start(), calls=%async_computation.5 | async-start | bytes 12582912 | tf_op jit(solution)/shard_map/all_gather | solution.py:223
  138.7 2.0 copy-start.3
  140.7 100.1 %all-to-all-start = ((bf16[16,128,1024]{2,1,0:T(8,128)(2,1)}), bf16[16,128,1024]{2,1,0:T(8,128)(2,1)}, u32[]{:S(2)}, u32[]{:S(2)}) async-start(bf16[16,128,1024]{2,1,0:T(8,128)(2,1)} %bitcast.53), calls=%async_computation | async-start | bytes 8388608 | tf_op jit(solution)/shard_map/all_to_all | solution.py:221
  154.7 3.4 copy-start.5
  159.5 86.2 %collective-permute-start = (bf16[128,4,8,128]{3,2,1,0:T(8,128)(2,1)}, bf16[128,4,8,128]{3,2,1,0:T(8,128)(2,1)S(1)}, u32[]{:S(2)}, u32[]{:S(2)}) collective-permute-start(bf16[128,4,8,128]{3,2,1,0:T(8,128)(2,1)} %get-tuple-element.7), channel_id=1, source_target_pairs={{0,1},{1,0},{2,3},{3,2},{4,5},{5,4},{6,7},{7,6},{8,9},{9,8},{10,11... | collective-permute-start | bytes 3145736 | tf_op jit(solution)/shard_map/ppermute | solution.py:185
  159.7 85.9 %collective-permute-start.1 = (bf16[128,4,8,128]{3,2,1,0:T(8,128)(2,1)S(1)}, bf16[128,4,8,128]{3,2,1,0:T(8,128)(2,1)S(1)}, u32[]{:S(2)}, u32[]{:S(2)}) collective-permute-start(bf16[128,4,8,128]{3,2,1,0:T(8,128)(2,1)S(1)} %get-tuple-element.8), channel_id=1, source_target_pairs={{0,1},{1,0},{2,3},{3,2},{4,5},{5,4},{6,7},{7,6},{8,9},{9,8},{10,11... | collective-permute-start | bytes 3145736 | tf_op jit(solution)/shard_map/ppermute | solution.py:185
  240.8 12.8 %copy-start.6 = (s32[2,8]{1,0:T(2,128)S(1)}, s32[2,8]{1,0:T(2,128)}, u32[]{:S(2)}) copy-start(s32[2,8]{1,0:T(2,128)} %param.12) | copy-start | bytes 196
  240.8 243.4 %all-to-all-start.3 = ((bf16[16,128,1024]{2,1,0:T(8,128)(2,1)}), bf16[16,128,1024]{2,1,0:T(8,128)(2,1)}, u32[]{:S(2)}, u32[]{:S(2)}) async-start(bf16[16,128,1024]{2,1,0:T(8,128)(2,1)} %bitcast.62), calls=%async_computation.3 | async-start | bytes 8388608 | tf_op jit(solution)/shard_map/all_to_all | solution.py:239
  246.6 95.1 %collective-permute-start.2 = (bf16[2,4,8,1280]{3,2,1,0:T(8,128)(2,1)S(1)}, bf16[2,4,8,1280]{3,2,1,0:T(8,128)(2,1)S(1)}, u32[]{:S(2)}, u32[]{:S(2)}) collective-permute-start(bf16[2,4,8,1280]{3,2,1,0:T(8,128)(2,1)S(1)} %get-tuple-element.5), channel_id=1, source_target_pairs={{0,2},{2,4},{4,6},{6,8},{8,10},{10,12},{12,14},{1,3},{3,5},{5,7},{... | collective-permute-start | bytes 491528 | tf_op jit(solution)/shard_map/ppermute | solution.py:185
  250.0 91.7 %collective-permute-start.3 = (bf16[2,4,8,1280]{3,2,1,0:T(8,128)(2,1)S(1)}, bf16[2,4,8,1280]{3,2,1,0:T(8,128)(2,1)S(1)}, u32[]{:S(2)}, u32[]{:S(2)}) collective-permute-start(bf16[2,4,8,1280]{3,2,1,0:T(8,128)(2,1)S(1)} %get-tuple-element.6), channel_id=1, source_target_pairs={{2,0},{4,2},{6,4},{8,6},{10,8},{12,10},{14,12},{3,1},{5,3},{7,5},{... | collective-permute-start | bytes 491528 | tf_op jit(solution)/shard_map/ppermute | solution.py:185
  253.7 99.0 %copy-start.4 = (f32[4]{0:T(128)S(1)}, f32[4]{0:T(128)}, u32[]{:S(2)}) copy-start(f32[4]{0:T(128)} %cour_ref.1) | copy-start | bytes 52
  444.4 8.2 %copy-start.7 = (bf16[1024,1024]{1,0:T(8,128)(2,1)S(1)}, bf16[1024,1024]{1,0:T(8,128)(2,1)}, u32[]{:S(2)}) copy-start(bf16[1024,1024]{1,0:T(8,128)(2,1)} %all-gather.3.cloned.1.call-done) | copy-start | bytes 6291460
  444.4 184.3 %collective-permute-start.4 = (bf16[128,4,8,1024]{3,2,1,0:T(8,128)(2,1)}, bf16[128,4,8,1024]{3,2,1,0:T(8,128)(2,1)}, u32[]{:S(2)}, u32[]{:S(2)}) collective-permute-start(bf16[128,4,8,1024]{3,2,1,0:T(8,128)(2,1)} %evolve.1), channel_id=1, source_target_pairs={{0,16},{1,17},{2,18},{3,19},{4,20},{5,21},{6,22},{7,23},{8,24},{9,... | collective-permute-start | bytes 25165832 | tf_op jit(solution)/shard_map/ppermute | solution.py:227
  484.2 158.0 %all-to-all-start.1 = ((bf16[16,128,1024]{2,1,0:T(8,128)(2,1)}), bf16[16,128,1024]{2,1,0:T(8,128)(2,1)}, u32[]{:S(2)}, u32[]{:S(2)}) async-start(bf16[16,128,1024]{2,1,0:T(8,128)(2,1)} %bitcast.63), calls=%async_computation.1 | async-start | bytes 8388608 | tf_op jit(solution)/shard_map/all_to_all | solution.py:239
  642.2 13.5 %copy-start.1 = (bf16[128,1024]{1,0:T(8,128)(2,1)S(1)}, bf16[128,1024]{1,0:T(8,128)(2,1)}, u32[]{:S(2)}) copy-start(bf16[128,1024]{1,0:T(8,128)(2,1)} %param.11) | copy-start | bytes 786436
Sparse Core Ops, SparseCore 0:
  133.5 24.1 all-gather.2
  159.2 21.0 all-gather.4

commit v2 on v0

--- a/solution.py
+++ b/solution.py
@@ -1,6 +1,8 @@
 import jax
 import jax.numpy as jnp
 from jax import lax
+from jax.experimental import pallas as pl
+from jax.experimental.pallas import tpu as pltpu
 from jax.sharding import PartitionSpec as P
 
 
@@ -43,7 +45,7 @@
     return (1.0 - blending) * field_now + blending * shifted
 
 
-def body(control, deviations, increments, lon_corr, lat_corr, offsets, courant):
+def lat_columns(control, deviations, increments, lon_corr, lat_corr, offsets, courant):
     lat_count = control.shape[0]
     lon_count = control.shape[4]
     flat_rows = control.reshape(-1, lon_count)
@@ -65,6 +67,397 @@
     return increments - previous - forcing
 
 
+LIMIT = 60 * 1024 * 1024
+
+
+def cost(flops, nbytes):
+    return pl.CostEstimate(flops=flops, bytes_accessed=nbytes, transcendentals=0)
+
+
+def row_block(rows, largest):
+    block = min(rows, largest)
+    while rows % block:
+        block -= 16
+    return block
+
+
+def residual(increments, deviations, previous, correlated, first, count, filled):
+    rows, nvar, levels, lons = increments.shape
+    block = row_block(rows, 32)
+
+    def kernel(inc_ref, dev_ref, prev_ref, corr_ref, *others):
+        out_ref = others[-1]
+        corr = jnp.swapaxes(corr_ref[0].astype(jnp.float32), 0, 1)
+        has_past = lax.axis_index("tm") > 0
+        previous = jnp.where(has_past, prev_ref[:, 0].astype(jnp.float32), 0.0)
+        out_ref[:, 0] = (
+            inc_ref[:, 0] - previous - dev_ref[:, 0] * corr
+        )
+
+    spec = pl.BlockSpec((block, 1, levels, lons), lambda v, r: (r, first + v, 0, 0))
+    in_specs = [spec] * 3 + [
+        pl.BlockSpec((1, levels, block, lons), lambda v, r: (v, 0, r, 0))
+    ]
+    operands = [increments, deviations, previous, correlated]
+    aliases = {}
+    if filled is not None:
+        in_specs.append(pl.BlockSpec(memory_space=pl.ANY))
+        operands.append(filled)
+        aliases = {4: 0}
+    return pl.pallas_call(
+        kernel,
+        grid=(count, rows // block),
+        in_specs=in_specs,
+        out_specs=spec,
+        out_shape=jax.ShapeDtypeStruct(increments.shape, jnp.float32),
+        input_output_aliases=aliases,
+        compiler_params=pltpu.CompilerParams(vmem_limit_bytes=LIMIT),
+        cost_estimate=cost(6 * count * levels * rows * lons, 16 * count * levels * rows * lons),
+        name="residual",
+    )(*operands)
+
+
+def swap(value, axis, steps, periodic):
+    count = lax.axis_size(axis)
+    pairs = [(i, i + steps) for i in range(count) if 0 <= i + steps < count]
+    if periodic:
+        pairs = [(i, (i + steps) % count) for i in range(count)]
+    return lax.ppermute(value, axis, pairs)
+
+
+def widen(field, rim):
+    low = swap(field[..., field.shape[-1] - rim :], "lon", 1, True)
+    high = swap(field[..., :rim], "lon", -1, True)
+    last = jnp.concatenate([low[-2:], field[-2:], high[-2:]], axis=-1)
+    first = jnp.concatenate([low[:2], field[:2], high[:2]], axis=-1)
+    return low, high, swap(last, "lat", 1, False), swap(first, "lat", -1, False)
+
+def exchange(control, increments, low, high, below, above, lon_corr, lat_corr, offsets, courant):
+    rows, nvar, levels, lons = control.shape
+    n_tm, n_lat, n_lon = (lax.axis_size(axis) for axis in ("tm", "lat", "lon"))
+    group = n_lat * n_lon
+    rounds = nvar * levels // group
+    vars_each = nvar // rounds
+    lats, width = n_lat * rows, n_lon * lons
+    rim = low.shape[-1]
+    wide = lons + 2 * rim
+    strip = lat_corr.shape[1] // (n_tm * n_lon)
+    row_tile = row_block(lats, 256)
+    lon_tile = row_block(width, 512)
+    bf16 = jnp.bfloat16
+
+    def kernel(
+        off_ref, cour_ref, ctl, inc, low_ref, high_ref, below_ref, above_ref, lonc, latc,
+        corr, prev,
+        stage, ctl_buf, whole, table, lat_table, smooth, pad, moved_buf,
+        load_sem, self_sem, lon_send, lon_recv, lat_send, lat_recv, tab_send, tab_recv,
+        out_send, out_recv, back_send, back_recv, tm_send, tm_recv,
+    ):
+        tm, la, lo = (lax.axis_index(axis) for axis in ("tm", "lat", "lon"))
+        me = la * n_lon + lo
+        strip_at = (tm * n_lon + lo) * strip
+
+        def at(index, size):
+            return pl.ds(pl.multiple_of(index * size, size), size)
+
+        def remote(src, dst, send, recv, tm_to, lat_to, lon_to):
+            return pltpu.make_async_remote_copy(
+                src_ref=src, dst_ref=dst, send_sem=send, recv_sem=recv,
+                device_id=(tm_to, lat_to, lon_to), device_id_type=pl.DeviceIdType.MESH,
+            )
+
+        def each_other(count, mine, do):
+            def step(i, carry):
+                pl.when(i != mine)(lambda: do(i))
+                return carry
+
+            lax.fori_loop(0, count, step, 0)
+
+        barrier = pltpu.get_barrier_semaphore()
+
+        def greet(tm_to, peer):
+            pl.semaphore_signal(
+                barrier, inc=1, device_id=(tm_to, peer // n_lon, peer % n_lon),
+                device_id_type=pl.DeviceIdType.MESH,
+            )
+
+        each_other(group, me, lambda peer: greet(tm, peer))
+        for lon_to in range(n_lon):
+            each_other(n_tm, tm, lambda other: greet(other, la * n_lon + lon_to))
+        pl.semaphore_wait(barrier, group - 1 + (n_tm - 1) * n_lon)
+
+        def outward(k, peer, origin):
+            return remote(
+                stage.at[k * group + peer],
+                whole.at[k, at(origin // n_lon, rows), at(origin % n_lon, lons)],
+                out_send.at[k, peer], out_recv.at[k, origin],
+                tm, peer // n_lon, peer % n_lon,
+            )
+
+        def homeward(k, peer, origin):
+            return remote(
+                whole.at[k, at(peer // n_lon, rows), at(peer % n_lon, lons)],
+                corr.at[k * group + origin],
+                back_send.at[k, peer], back_recv.at[k, origin],
+                tm, peer // n_lon, peer % n_lon,
+            )
+
+        def lon_share(lon_to, origin):
+            return remote(
+                lonc, table.at[at(origin, lons)],
+                lon_send.at[lon_to], lon_recv.at[origin], tm, la, lon_to,
+            )
+
+        def lat_share(lat_to, origin):
+            columns = at(tm * n_lon + lo, strip)
+            return remote(
+                latc.at[:, columns], lat_table.at[at(origin, rows), columns],
+                lat_send.at[lat_to], lat_recv.at[origin], tm, lat_to, lo,
+            )
+
+        def strip_share(other, origin):
+            return remote(
+                lat_table.at[:, at(tm * n_lon + lo, strip)],
+                lat_table.at[:, at(tm * n_lon + lo, strip)],
+                tab_send.at[other], tab_recv.at[origin], other // n_lon, la, other % n_lon,
+            )
+
+        def strip_arrival(origin):
+            return remote(
+                lat_table.at[:, at(origin, strip)], lat_table.at[:, at(origin, strip)],
+                tab_send.at[origin], tab_recv.at[origin], origin // n_lon, la, origin % n_lon,
+            )
+
+        def own(k):
+            return pltpu.make_async_copy(
+                stage.at[k * group + me], whole.at[k, at(la, rows), at(lo, lons)],
+                self_sem.at[k],
+            )
+
+        def own_back(k):
+            return pltpu.make_async_copy(
+                whole.at[k, at(la, rows), at(lo, lons)], corr.at[k * group + me],
+                self_sem.at[rounds + k],
+            )
+
+        def own_tables():
+            columns = at(tm * n_lon + lo, strip)
+            return (
+                pltpu.make_async_copy(lonc, table.at[at(lo, lons)], load_sem.at[0]),
+                pltpu.make_async_copy(
+                    latc.at[:, columns], lat_table.at[at(la, rows), columns], load_sem.at[1]
+                ),
+            )
+
+        def send_out(k):
+            far = (me * vars_each // group + vars_each // 2) % vars_each
+            for t in range(vars_each):
+                local = (far + t) % vars_each
+                load = pltpu.make_async_copy(
+                    ctl.at[:, k * vars_each + local], ctl_buf, load_sem.at[2]
+                )
+                load.start()
+                load.wait()
+
+                def turn(r, carry):
+                    part = ctl_buf[pl.ds(r * 16, 16)].astype(jnp.float32)
+                    first = (k * vars_each + local) * levels
+                    stage[pl.ds(first, levels), pl.ds(r * 16, 16), :] = jnp.swapaxes(
+                        part, 0, 1
+                    ).astype(bf16)
+                    return carry
+
+                lax.fori_loop(0, rows // 16, turn, 0)
+
+                def send(l, carry):
+                    peer = local * levels + l
+                    pl.when(peer != me)(lambda: outward(k, peer, me).start())
+                    return carry
+
+                lax.fori_loop(0, levels, send, 0)
+            own(k).start()
+
+        def advect(v):
+            body_rows = pl.ds(2, rows)
+            loads = [
+                pltpu.make_async_copy(
+                    inc.at[:, v], pad.at[body_rows, :, pl.ds(rim, lons)], load_sem.at[3]
+                ),
+                pltpu.make_async_copy(
+                    low_ref.at[:, v], pad.at[body_rows, :, pl.ds(0, rim)], load_sem.at[4]
+                ),
+                pltpu.make_async_copy(
+                    high_ref.at[:, v], pad.at[body_rows, :, pl.ds(rim + lons, rim)],
+                    load_sem.at[5],
+                ),
+                pltpu.make_async_copy(below_ref.at[:, v], pad.at[pl.ds(0, 2)], load_sem.at[6]),
+                pltpu.make_async_copy(
+                    above_ref.at[:, v], pad.at[pl.ds(2 + rows, 2)], load_sem.at[7]
+                ),
+            ]
+            for load in loads:
+                load.start()
+            for load in loads:
+                load.wait()
+            weight = cour_ref[v]
+            lat_off, lon_off = off_ref[:, 0:1], off_ref[:, 1:2]
+
+            def one(i):
+                row = pad[i + 2]
+                centre = row[:, rim : rim + lons]
+                for step in (-2, -1, 1, 2):
+                    row = jnp.where(lat_off == step, pad[i + 2 - step], row)
+                moved = row[:, rim : rim + lons]
+                for step in (-2, -1, 1, 2):
+                    rolled = pltpu.roll(row, step % wide, 1)[:, rim : rim + lons]
+                    moved = jnp.where(lon_off == step, rolled, moved)
+                mixed = (1.0 - weight) * centre + weight * moved
+                moved_buf[v, i] = mixed.astype(bf16)
+
+            def pair(i, carry):
+                one(2 * i)
+                one(2 * i + 1)
+                return carry
+
+            lax.fori_loop(0, rows // 2, pair, 0)
+            onward(v).start()
+
+        def onward(v):
+            return remote(
+                moved_buf.at[v], prev.at[:, v], tm_send.at[v], tm_recv.at[v],
+                (tm + 1) % n_tm, la, lo,
+            )
+
+        def correlate(k):
+            def smooth_tile(i, carry):
+                at_rows = at(i // (width // lon_tile), row_tile)
+                at_lons = at(i % (width // lon_tile), lon_tile)
+                smooth[at_rows, at_lons] = lax.dot_general(
+                    whole[k, at_rows, :], table[at_lons, :], (((1,), (1,)), ((), ())),
+                    preferred_element_type=jnp.float32,
+                ).astype(bf16)
+                return carry
+
+            lax.fori_loop(0, (lats // row_tile) * (width // lon_tile), smooth_tile, 0)
+            if k == 0:
+                each_other(n_tm * n_lon, tm * n_lon + lo, lambda s: strip_arrival(s).wait_recv())
+
+            def tile(i, carry):
+                peer = (me + group // 2 + i) % group
+                at_rows, at_lons = at(peer // n_lon, rows), at(peer % n_lon, lons)
+                whole[k, at_rows, at_lons] = jnp.dot(
+                    lat_table[at_rows, :], smooth[:, at_lons],
+                    preferred_element_type=jnp.float32,
+                ).astype(bf16)
+                pl.when(peer != me)(lambda: homeward(k, peer, me).start())
+                return carry
+
+            lax.fori_loop(0, group, tile, 0)
+            own_back(k).start()
+
+        send_out(0)
+        for load in own_tables():
+            load.start()
+        each_other(n_lat, la, lambda p: lat_share(p, la).start())
+        each_other(n_lon, lo, lambda p: lon_share(p, lo).start())
+        half = nvar // 2
+        for v in range(half):
+            advect(v)
+        for k in range(1, rounds):
+            send_out(k)
+        for load in own_tables():
+            load.wait()
+        each_other(n_lat, la, lambda s: lat_share(s, s).wait_recv())
+        each_other(n_tm * n_lon, tm * n_lon + lo, lambda p: strip_share(p, tm * n_lon + lo).start())
+        for v in range(half, nvar):
+            advect(v)
+        each_other(n_lon, lo, lambda s: lon_share(s, s).wait_recv())
+        for k in range(rounds):
+            own(k).wait()
+            each_other(group, me, lambda s: outward(k, s, s).wait_recv())
+            correlate(k)
+        each_other(n_lat, la, lambda p: lat_share(p, la).wait_send())
+        each_other(n_lon, lo, lambda p: lon_share(p, lo).wait_send())
+        each_other(
+            n_tm * n_lon, tm * n_lon + lo, lambda p: strip_share(p, tm * n_lon + lo).wait_send()
+        )
+        for v in range(nvar):
+            onward(v).wait()
+        for k in range(rounds):
+            own_back(k).wait()
+            each_other(group, me, lambda p: outward(k, p, me).wait_send())
+            each_other(group, me, lambda p: homeward(k, p, me).wait_send())
+            each_other(group, me, lambda s: homeward(k, s, s).wait_recv())
+
+    hbm = pl.BlockSpec(memory_space=pl.ANY)
+    dma = pltpu.SemaphoreType.DMA
+    n_strips = n_tm * n_lon
+    return pl.pallas_call(
+        kernel,
+        in_specs=[
+            pl.BlockSpec(memory_space=pltpu.VMEM),
+            pl.BlockSpec(memory_space=pltpu.SMEM),
+        ] + [hbm] * 8,
+        out_specs=[hbm, hbm],
+        out_shape=[
+            jax.ShapeDtypeStruct((nvar * levels, rows, lons), bf16),
+            jax.ShapeDtypeStruct((rows, nvar, levels, lons), bf16),
+        ],
+        scratch_shapes=[
+            pltpu.VMEM((nvar * levels, rows, lons), bf16),
+            pltpu.VMEM((rows, levels, lons), bf16),
+            pltpu.VMEM((rounds, lats, width), bf16),
+            pltpu.VMEM((width, width), bf16),
+            pltpu.VMEM((lats, lats), bf16),
+            pltpu.VMEM((lats, width), bf16),
+            pltpu.VMEM((rows + 4, levels, wide), jnp.float32),
+            pltpu.VMEM((nvar, rows, levels, lons), bf16),
+            dma((8,)), dma((2 * rounds,)),
+            dma((n_lon,)), dma((n_lon,)), dma((n_lat,)), dma((n_lat,)),
+            dma((n_strips,)), dma((n_strips,)),
+            dma((rounds, group)), dma((rounds, group)),
+            dma((rounds, group)), dma((rounds, group)),
+            dma((nvar,)), dma((nvar,)),
+        ],
+        compiler_params=pltpu.CompilerParams(
+            vmem_limit_bytes=LIMIT, collective_id=0, has_side_effects=True
+        ),
+        cost_estimate=cost(2 * rounds * lats * width * (lats + width), 12 * control.size),
+        name="exchange",
+    )(offsets.T, courant, control, increments, low, high, below, above, lon_corr, lat_corr)
+
+
+def whole_fields(control, deviations, increments, lon_corr, lat_corr, offsets, courant):
+    rows, _, nvar, levels, lons = control.shape
+    flat = (rows, nvar, levels, lons)
+    control, deviations, increments = (
+        x.reshape(flat) for x in (control, deviations, increments)
+    )
+    rims = widen(increments, 128)
+    correlated, previous = exchange(
+        control, increments, *rims, lon_corr, lat_corr, offsets, courant
+    )
+    correlated = correlated.reshape(nvar, levels, rows, lons)
+    out = residual(increments, deviations, previous, correlated, 0, nvar, None)
+    return out.reshape(rows, 1, nvar, levels, lons)
+
+
+def body(control, deviations, increments, lon_corr, lat_corr, offsets, courant):
+    rows, slots, nvar, levels, lons = control.shape
+    group = lax.axis_size("lat") * lax.axis_size("lon")
+    sharers = lax.axis_size("tm") * lax.axis_size("lon")
+    arrays = (control, deviations, increments, lon_corr, lat_corr, offsets, courant)
+    fits = (
+        slots == 1
+        and (nvar * levels) % group == 0
+        and group % levels == 0
+        and rows % 16 == 0
+        and lons % 128 == 0
+        and lat_corr.shape[1] % (128 * sharers) == 0
+    )
+    return whole_fields(*arrays) if fits else lat_columns(*arrays)
+
+
 def solution(mesh):
     in_specs = (
         P("lat", "tm", None, None, "lon"),

time: 1230 us -> 449 us (0.37)
  waiting for transfers between devices: 813 us -> 17.6 us
  Pallas kernels: 0 us -> 413 us
  local copies, waits for them, and re-layouts: 243 us -> 5.18 us
  other arithmetic: 69.4 us -> 0.05 us
  matrix products: 39.6 us -> 0 us
  between operations: 34.7 us -> 0.09 us
  starting transfers between devices: 23.9 us -> 7.31 us
    ppermute x5 -> x4, waiting for transfers between devices: 573 us -> 17.6 us  [swap(): return lax.ppermute(value, axis, pairs)]
    pallas_call x0 -> x2, Pallas kernels: none -> 413 us  [the longest x1 387 us: exchange(): pl.pallas_call(kernel, in_specs=[pl.BlockSpec(memory_space=pltpu.VMEM), p...]
    all_gather x2 -> x0, waiting for transfers between devices: 203 us -> none  [the longest x1 170 us: body(): full_table = lax.all_gather(lat_corr, 'lat', axis=0, tiled=True)]
    unnamed x23 -> x11, local copies, waits for them, and re-layouts: 63.3 us -> 1.42 us
    concatenate x1 -> x0, local copies, waits for them, and re-layouts: 54.5 us -> none  [with_halo(): block = jnp.concatenate([low, block, high], axis=dim)]
    slice x8 -> x4, local copies, waits for them, and re-layouts: 50.2 us -> 3.77 us  [the longest x1 2.69 us: widen(): high = swap(field[..., :rim], 'lon', -1, True)]
    all_to_all x3 -> x0, local copies, waits for them, and re-layouts: 42.7 us -> none  [the longest x2 25.3 us: body(): lax.all_to_all(halfway, 'lat', split_axis=1, concat_axis=0, tiled=True)]
    dot_general x2 -> x0, matrix products: 39.7 us -> none  [the longest x1 23.5 us: body(): lax.dot_general(lax.all_gather(flat_rows, 'lon', axis=1, tiled=True), lon...]
  transfers between devices with their start and end apart: 9 -> 4, of which waited for: 5 -> 4; matrix products, arithmetic and copies ran while one was open for 18% -> 0% of each run, Pallas kernels for 0% -> 0%
where the time goes in v2:
time: 449 us; the launch traced here: 444 us
  Pallas kernels  413 us (92%)
  waiting for transfers between devices  17.6 us (4%)
  starting transfers between devices  7.31 us (2%)
  local copies, waits for them, and re-layouts  5.18 us (1%)
    pallas_call x1, Pallas kernels, exchange(): pl.pallas_call(kernel, in_specs=[pl.BlockSpec(memory_space=pltpu.VMEM), p...  387 us
    pallas_call x1, Pallas kernels, residual(): pl.pallas_call(kernel, grid=(count, rows // block), in_specs=in_specs, ou...  26.2 us
    ppermute x4, waiting for transfers between devices, swap(): return lax.ppermute(value, axis, pairs)  17.6 us
  transfers between devices with their start and end apart: 4, of which 4 were waited for; matrix products, arithmetic and copies ran while one was open for 0% of the time, Pallas kernels for 0%

profile of v2, /device:TPU:18, one launch (start us, length us, event | category | flops | bytes accessed | tf_op | source)
XLA Modules:
  0.0 443.7 jit_solution(6666392421648110874)
XLA Ops:
  0.0 0.0 copy-start.2
  0.0 2.7 fusion
  2.7 0.1 collective-permute-start.1
  2.8 0.5 collective-permute-start
  3.3 1.1 slice_bitcast_fusion
  4.3 2.6 collective-permute-done.1.high_ref
  6.9 0.0 copy-start
  6.9 3.0 collective-permute-done.low_ref
  9.9 0.0 copy-start.1
  10.0 3.4 collective-permute-start.2
  13.4 0.0 copy-done.1
  13.4 3.3 collective-permute-start.3
  16.8 0.0 copy-done.2
  16.8 0.7 copy.8
  17.4 10.2 %collective-permute-done.2.below_ref = f32[2,4,8,1280]{3,2,1,0:T(8,128)S(1)} collective-permute-done((f32[2,4,8,1280]{3,2,1,0:T(8,128)S(1)}, f32[2,4,8,1280]{3,2,1,0:T(8,128)S(1)}, u32[]{:S(2)}, u32[]{:S(2)}) %collective-permute-start.2) | collective-permute-done | bytes 327712 | tf_op jit(solution)/shard_map/ppermute | solution.py:125
  27.7 0.0 copy-start.3
  27.7 1.9 collective-permute-done.3.above_ref
  29.5 0.0 copy-start.4
  29.5 0.0 copy-done
  29.5 0.0 copy-done.3
  29.5 0.7 copy-done.4
  30.3 387.3 %exchange.1 = (bf16[32,128,1024]{2,1,0:T(8,128)(2,1)}, bf16[128,4,8,1024]{3,2,1,0:T(8,128)(2,1)}) custom-call(s32[8,2]{1,0:T(8,128)} %bitcast.19, f32[4]{0:T(128)} %cour_ref.1, bf16[128,4,8,1024]{3,2,1,0:T(8,128)(2,1)} %bitcast.20, f32[128,4,8,1024]{3,2,1,0:T(8,128)} %bitcast.15, f32[128,4,8,128]{3,2,1,0:T(8,128)} %copy-done.1, f32[128,4,8,128]{3,2,1,0:T(8,128)} %copy-done, ...), custom_call_target="tpu_custom_call" | custom-call | flops 25769803776 | bytes 50331648 | tf_op jit(solution)/shard_map/exchange/pallas_call | solution.py:395
  417.5 26.2 %residual.1 = f32[128,4,8,1024]{3,2,1,0:T(8,128)} custom-call(f32[128,4,8,1024]{3,2,1,0:T(8,128)} %bitcast.16, f32[128,4,8,1024]{3,2,1,0:T(8,128)} %bitcast.17, bf16[128,4,8,1024]{3,2,1,0:T(8,128)(2,1)} %get-tuple-element.7.prev_ref, bf16[4,8,128,1024]{3,2,1,0:T(8,128)(2,1)} %bitcast.18), custom_call_target="tpu_custom_call" | custom-call | flops 25165824 | bytes 67108864 | tf_op jit(solution)/shard_map/residual/pallas_call | solution.py:107
  (4 shorter events, 0.1 us)
Async XLA Ops:
  0.0 16.8 %copy-start.2 = (s32[2,8]{1,0:T(2,128)S(1)}, s32[2,8]{1,0:T(2,128)}, u32[]{:S(2)}) copy-start(s32[2,8]{1,0:T(2,128)} %param.12) | copy-start | bytes 196
  2.7 4.2 collective-permute-start.1
  2.8 7.1 %collective-permute-start = (f32[128,4,8,128]{3,2,1,0:T(8,128)S(1)}, f32[128,4,8,128]{3,2,1,0:T(8,128)S(1)}, u32[]{:S(2)}, u32[]{:S(2)}) collective-permute-start(f32[128,4,8,128]{3,2,1,0:T(8,128)S(1)} %get-tuple-element.12), channel_id=1, source_target_pairs={{0,1},{1,0},{2,3},{3,2},{4,5},{5,4},{6,7},{7,6},{8,9},{9,8},{10,11... | collective-permute-start | bytes 6291464 | tf_op jit(solution)/shard_map/ppermute | solution.py:125
  6.9 22.6 %copy-start = (f32[128,4,8,128]{3,2,1,0:T(8,128)}, f32[128,4,8,128]{3,2,1,0:T(8,128)S(1)}, u32[]{:S(2)}) copy-start(f32[128,4,8,128]{3,2,1,0:T(8,128)S(1)} %collective-permute-done.1.high_ref) | copy-start | bytes 6291460
  9.9 3.5 copy-start.1
  10.0 17.7 %collective-permute-start.2 = (f32[2,4,8,1280]{3,2,1,0:T(8,128)S(1)}, f32[2,4,8,1280]{3,2,1,0:T(8,128)S(1)}, u32[]{:S(2)}, u32[]{:S(2)}) collective-permute-start(f32[2,4,8,1280]{3,2,1,0:T(8,128)S(1)} %pad_maximum_fusion), channel_id=1, source_target_pairs={{0,2},{2,4},{4,6},{6,8},{8,10},{10,12},{12,14},{1,3},{3,5},{5,7},{... | collective-permute-start | bytes 983048 | tf_op jit(solution)/shard_map/ppermute | solution.py:125
  13.4 16.1 %collective-permute-start.3 = (f32[2,4,8,1280]{3,2,1,0:T(8,128)S(1)}, f32[2,4,8,1280]{3,2,1,0:T(8,128)S(1)}, u32[]{:S(2)}, u32[]{:S(2)}) collective-permute-start(f32[2,4,8,1280]{3,2,1,0:T(8,128)S(1)} %pad_maximum_fusion.1), channel_id=1, source_target_pairs={{2,0},{4,2},{6,4},{8,6},{10,8},{12,10},{14,12},{3,1},{5,3},{7,5},{... | collective-permute-start | bytes 983048 | tf_op jit(solution)/shard_map/ppermute | solution.py:125
  27.7 1.9 copy-start.3
  29.5 0.7 copy-start.4

commit v3 on v2

--- a/solution.py
+++ b/solution.py
@@ -117,29 +117,14 @@
     )(*operands)
 
 
-def swap(value, axis, steps, periodic):
-    count = lax.axis_size(axis)
-    pairs = [(i, i + steps) for i in range(count) if 0 <= i + steps < count]
-    if periodic:
-        pairs = [(i, (i + steps) % count) for i in range(count)]
-    return lax.ppermute(value, axis, pairs)
-
-
-def widen(field, rim):
-    low = swap(field[..., field.shape[-1] - rim :], "lon", 1, True)
-    high = swap(field[..., :rim], "lon", -1, True)
-    last = jnp.concatenate([low[-2:], field[-2:], high[-2:]], axis=-1)
-    first = jnp.concatenate([low[:2], field[:2], high[:2]], axis=-1)
-    return low, high, swap(last, "lat", 1, False), swap(first, "lat", -1, False)
-
-def exchange(control, increments, low, high, below, above, lon_corr, lat_corr, offsets, courant):
+def exchange(control, increments, lon_corr, lat_corr, offsets, courant):
     rows, nvar, levels, lons = control.shape
     n_tm, n_lat, n_lon = (lax.axis_size(axis) for axis in ("tm", "lat", "lon"))
     group = n_lat * n_lon
     rounds = nvar * levels // group
     vars_each = nvar // rounds
     lats, width = n_lat * rows, n_lon * lons
-    rim = low.shape[-1]
+    rim = 128
     wide = lons + 2 * rim
     strip = lat_corr.shape[1] // (n_tm * n_lon)
     row_tile = row_block(lats, 256)
@@ -147,11 +132,12 @@
     bf16 = jnp.bfloat16
 
     def kernel(
-        off_ref, cour_ref, ctl, inc, low_ref, high_ref, below_ref, above_ref, lonc, latc,
-        corr, prev,
+        off_ref, cour_ref, ctl, inc, lonc, latc,
+        corr, prev, low_ref, high_ref, below_ref, above_ref,
         stage, ctl_buf, whole, table, lat_table, smooth, pad, moved_buf,
         load_sem, self_sem, lon_send, lon_recv, lat_send, lat_recv, tab_send, tab_recv,
         out_send, out_recv, back_send, back_recv, tm_send, tm_recv,
+        side_send, side_recv, edge_send, edge_recv,
     ):
         tm, la, lo = (lax.axis_index(axis) for axis in ("tm", "lat", "lon"))
         me = la * n_lon + lo
@@ -185,6 +171,67 @@
         for lon_to in range(n_lon):
             each_other(n_tm, tm, lambda other: greet(other, la * n_lon + lon_to))
         pl.semaphore_wait(barrier, group - 1 + (n_tm - 1) * n_lon)
+
+        left, right = (lo + n_lon - 1) % n_lon, (lo + 1) % n_lon
+        centre_lanes, low_lanes, high_lanes = (
+            pl.ds(rim, lons), pl.ds(0, rim), pl.ds(rim + lons, rim)
+        )
+
+        def sides():
+            return (
+                remote(
+                    inc.at[:, :, :, pl.ds(lons - rim, rim)], low_ref,
+                    side_send.at[0], side_recv.at[0], tm, la, right,
+                ),
+                remote(
+                    inc.at[:, :, :, pl.ds(0, rim)], high_ref,
+                    side_send.at[1], side_recv.at[1], tm, la, left,
+                ),
+            )
+
+        def edges(way):
+            first, dst, lat_to = ((rows - 2, below_ref, la + 1), (0, above_ref, la - 1))[way]
+            parts = (
+                (pl.ds(0, lons), centre_lanes, lo),
+                (pl.ds(lons - rim, rim), low_lanes, right),
+                (pl.ds(0, rim), high_lanes, left),
+            )
+            return [
+                remote(
+                    inc.at[pl.ds(first, 2), :, :, src_lanes], dst.at[:, :, :, dst_lanes],
+                    edge_send.at[3 * way + i], edge_recv.at[3 * way + i], tm, lat_to, lon_to,
+                )
+                for i, (src_lanes, dst_lanes, lon_to) in enumerate(parts)
+            ]
+
+        has_below, has_above = la > 0, la < n_lat - 1
+
+        def start_rims():
+            for copy in sides():
+                copy.start()
+            for way, may_send in enumerate((has_above, has_below)):
+
+                @pl.when(may_send)
+                def _():
+                    for copy in edges(way):
+                        copy.start()
+
+        def wait_rims():
+            for copy in sides():
+                copy.wait()
+            for way, (may_send, may_get) in enumerate(
+                ((has_above, has_below), (has_below, has_above))
+            ):
+
+                @pl.when(may_send)
+                def _():
+                    for copy in edges(way):
+                        copy.wait_send()
+
+                @pl.when(may_get)
+                def _():
+                    for copy in edges(way):
+                        copy.wait_recv()
 
         def outward(k, peer, origin):
             return remote(
@@ -290,13 +337,25 @@
                     high_ref.at[:, v], pad.at[body_rows, :, pl.ds(rim + lons, rim)],
                     load_sem.at[5],
                 ),
-                pltpu.make_async_copy(below_ref.at[:, v], pad.at[pl.ds(0, 2)], load_sem.at[6]),
-                pltpu.make_async_copy(
-                    above_ref.at[:, v], pad.at[pl.ds(2 + rows, 2)], load_sem.at[7]
-                ),
             ]
             for load in loads:
                 load.start()
+            for present, ref, first, sem in (
+                (has_below, below_ref, 0, 6), (has_above, above_ref, 2 + rows, 7)
+            ):
+
+                @pl.when(present)
+                def _():
+                    load = pltpu.make_async_copy(
+                        ref.at[:, v], pad.at[pl.ds(first, 2)], load_sem.at[sem]
+                    )
+                    load.start()
+                    load.wait()
+
+                @pl.when(jnp.logical_not(present))
+                def _():
+                    pad[pl.ds(first, 2)] = jnp.zeros((2, levels, wide), jnp.float32)
+
             for load in loads:
                 load.wait()
             weight = cour_ref[v]
@@ -355,12 +414,14 @@
             lax.fori_loop(0, group, tile, 0)
             own_back(k).start()
 
+        start_rims()
         send_out(0)
         for load in own_tables():
             load.start()
         each_other(n_lat, la, lambda p: lat_share(p, la).start())
         each_other(n_lon, lo, lambda p: lon_share(p, lo).start())
         half = nvar // 2
+        wait_rims()
         for v in range(half):
             advect(v)
         for k in range(1, rounds):
@@ -397,11 +458,15 @@
         in_specs=[
             pl.BlockSpec(memory_space=pltpu.VMEM),
             pl.BlockSpec(memory_space=pltpu.SMEM),
-        ] + [hbm] * 8,
-        out_specs=[hbm, hbm],
+        ] + [hbm] * 4,
+        out_specs=[hbm] * 6,
         out_shape=[
             jax.ShapeDtypeStruct((nvar * levels, rows, lons), bf16),
             jax.ShapeDtypeStruct((rows, nvar, levels, lons), bf16),
+            jax.ShapeDtypeStruct((rows, nvar, levels, rim), jnp.float32),
+            jax.ShapeDtypeStruct((rows, nvar, levels, rim), jnp.float32),
+            jax.ShapeDtypeStruct((2, nvar, levels, wide), jnp.float32),
+            jax.ShapeDtypeStruct((2, nvar, levels, wide), jnp.float32),
         ],
         scratch_shapes=[
             pltpu.VMEM((nvar * levels, rows, lons), bf16),
@@ -418,13 +483,14 @@
             dma((rounds, group)), dma((rounds, group)),
             dma((rounds, group)), dma((rounds, group)),
             dma((nvar,)), dma((nvar,)),
+            dma((2,)), dma((2,)), dma((6,)), dma((6,)),
         ],
         compiler_params=pltpu.CompilerParams(
             vmem_limit_bytes=LIMIT, collective_id=0, has_side_effects=True
         ),
         cost_estimate=cost(2 * rounds * lats * width * (lats + width), 12 * control.size),
         name="exchange",
-    )(offsets.T, courant, control, increments, low, high, below, above, lon_corr, lat_corr)
+    )(offsets.T, courant, control, increments, lon_corr, lat_corr)[:2]
 
 
 def whole_fields(control, deviations, increments, lon_corr, lat_corr, offsets, courant):
@@ -433,9 +499,8 @@
     control, deviations, increments = (
         x.reshape(flat) for x in (control, deviations, increments)
     )
-    rims = widen(increments, 128)
     correlated, previous = exchange(
-        control, increments, *rims, lon_corr, lat_corr, offsets, courant
+        control, increments, lon_corr, lat_corr, offsets, courant
     )
     correlated = correlated.reshape(nvar, levels, rows, lons)
     out = residual(increments, deviations, previous, correlated, 0, nvar, None)
@@ -449,6 +514,9 @@
     arrays = (control, deviations, increments, lon_corr, lat_corr, offsets, courant)
     fits = (
         slots == 1
+        and lax.axis_size("lat") > 1
+        and lax.axis_size("lon") > 1
+        and lax.axis_size("tm") > 1
         and (nvar * levels) % group == 0
         and group % levels == 0
         and rows % 16 == 0

time: 449 us -> 427 us (0.951)
  waiting for transfers between devices: 17.6 us -> 0 us
  starting transfers between devices: 7.31 us -> 0 us
  Pallas kernels: 413 us -> 420 us
    ppermute x4 -> x0, waiting for transfers between devices: 17.6 us -> none  [swap(): return lax.ppermute(value, axis, pairs)]
    ppermute x4 -> x0, starting transfers between devices: 7.31 us -> none  [swap(): return lax.ppermute(value, axis, pairs)]
    pallas_call x1, Pallas kernels: 387 us -> 394 us  [exchange(): pl.pallas_call(kernel, in_specs=[pl.BlockSpec(memory_space=pltpu.VMEM), p...]
  transfers between devices with their start and end apart: 4 -> 0, of which waited for: 4 -> 0; matrix products, arithmetic and copies ran while one was open for 0% -> 0% of each run, Pallas kernels for 0% -> 0%
where the time goes in v3:
time: 427 us; the launch traced here: 422 us
  Pallas kernels  420 us (98%)
    pallas_call x1, Pallas kernels, exchange(): pl.pallas_call(kernel, in_specs=[pl.BlockSpec(memory_space=pltpu.VMEM), p...  394 us
    pallas_call x1, Pallas kernels, residual(): pl.pallas_call(kernel, grid=(count, rows // block), in_specs=in_specs, ou...  26.2 us

profile of v3, /device:TPU:18, one launch (start us, length us, event | category | flops | bytes accessed | tf_op | source)
XLA Modules:
  0.0 421.7 jit_solution(5109871727526142144)
XLA Ops:
  0.0 1.3 copy.8
  1.3 394.2 %exchange.1 = (bf16[32,128,1024]{2,1,0:T(8,128)(2,1)}, bf16[128,4,8,1024]{3,2,1,0:T(8,128)(2,1)}, f32[128,4,8,128]{3,2,1,0:T(8,128)}, f32[128,4,8,128]{3,2,1,0:T...) custom-call(s32[8,2]{1,0:T(8,128)} %bitcast.12, f32[4]{0:T(128)} %cour_ref.1, ...), custom_call_target="tpu_custom_call" | custom-call | flops 25769803776 | bytes 50331648 | tf_op jit(solution)/shard_map/exchange/pallas_call | solution.py:456
  395.5 26.2 %residual.1 = f32[128,4,8,1024]{3,2,1,0:T(8,128)} custom-call(f32[128,4,8,1024]{3,2,1,0:T(8,128)} %bitcast.9, f32[128,4,8,1024]{3,2,1,0:T(8,128)} %bitcast.10, bf16[128,4,8,1024]{3,2,1,0:T(8,128)(2,1)} %get-tuple-element.7.prev_ref, bf16[4,8,128,1024]{3,2,1,0:T(8,128)(2,1)} %bitcast.11), custom_call_target="tpu_custom_call" | custom-call | flops 25165824 | bytes 67108864 | tf_op jit(solution)/shard_map/residual/pallas_call | solution.py:107
